TPU v7x, 32 devices: a whole 2x2x4 slice. The times are simulated.
32 devices in a mesh: ep: 4 (over z), et: 4 (over x, core), rep: 2 (over y).
Axes of the slice: x: 2, y: 2, z: 4, core: 2. Of those that a mesh axis runs over, the one named last changes fastest.
Arguments:
- grad_out: bfloat16 [2048, 7168], P(('ep', 'rep'), 'et'), may hold values from -6 to 6
- combine: float32 [2048, 2], P(('ep', 'rep')), may hold values from 0.1 to 1
- routing: int32 [2048, 2], P(('ep', 'rep')), may hold values from 0 to 3, all different within a row; in each aligned block of 256 rows (0 to 255, 256 to 511, ...) at most 192 rows name the same one
- expert_down_matrix: bfloat16 [4, 7168, 1024], P('ep', 'et'), may hold values from -0.0625 to 0.0625
- gate_pre: bfloat16 [4, 2, 1024, 768], P('ep', 'rep', 'et'), may hold values from -6 to 6
- up_pre: bfloat16 [4, 2, 1024, 768], P('ep', 'rep', 'et'), may hold values from -6 to 6
Outputs:
- grad_gate: bfloat16 [4, 2, 1024, 768], P('ep', 'rep', 'et')
- up_projection_gradient: bfloat16 [4, 2, 1024, 768], P('ep', 'rep', 'et')
- grad_down: bfloat16 [4, 7168, 1024], P('ep', ('et', 'rep'))
Inputs may be any that keep to these rules, and one draw needn't show every extreme that they name: `routing`: each row names 2 different experts. Among the 256 rows of one token group (aligned blocks), no expert is named more than 192 times, a bound that some block reaches.
All inputs are finite; a program needn't handle non-finite values.
Results may differ from a plain program's by a relative error of at most 0.015.
Values may be sent and summed in bfloat16 or wider, within the bound.
A program may use at most 64 MiB of HBM per device.

v0:
```python
import jax
import jax.numpy as jnp
from jax import lax
from jax.sharding import PartitionSpec as P


def local(grad_out, combine, routing, expert_down_matrix, gate_pre, up_pre):
    expert_count = lax.axis_size("ep")
    slot_count = gate_pre.shape[-1]
    capacity = slot_count // expert_count
    tok_rows, feat_cols = grad_out.shape
    pair_width = routing.shape[1]
    pair_total = tok_rows * pair_width
    targets = routing.reshape(pair_total)
    onehot = (targets[:, None] == jnp.arange(expert_count, dtype=jnp.int32)[None, :]).astype(
        jnp.int32
    )
    ranking = jnp.sum(
        (jnp.cumsum(onehot, axis=0, dtype=jnp.int32) - onehot) * onehot, axis=1, dtype=jnp.int32
    )
    destination = targets * capacity + ranking
    matches = destination[None, :] == jnp.arange(slot_count, dtype=jnp.int32)[:, None]
    filled = jnp.any(matches, axis=1)
    source_pair = jnp.sum(
        jnp.where(matches, jnp.arange(pair_total, dtype=jnp.int32)[None, :], 0),
        axis=1,
        dtype=jnp.int32,
    )
    weighted = (
        (grad_out.astype(jnp.float32)[:, None, :] * combine[:, :, None])
        .reshape(pair_total, feat_cols)
        .astype(jnp.bfloat16)
    )
    outgoing = jnp.where(
        filled[:, None], jnp.take(weighted, source_pair, axis=0), jnp.zeros((), jnp.bfloat16)
    )
    outgoing = outgoing.reshape(expert_count, capacity, feat_cols)
    incoming = lax.all_to_all(outgoing, "ep", split_axis=0, concat_axis=0, tiled=True).reshape(
        slot_count, feat_cols
    )
    weight_rows = expert_down_matrix[0]
    act_grad = lax.psum_scatter(
        lax.dot_general(
            weight_rows, incoming, (((0,), (1,)), ((), ())), preferred_element_type=jnp.float32
        ).astype(jnp.bfloat16),
        "et",
        scatter_dimension=0,
        tiled=True,
    ).astype(jnp.float32)
    gate_activation_values = gate_pre[0, 0].astype(jnp.float32)
    up_vals = up_pre[0, 0].astype(jnp.float32)
    gate_sig = jax.nn.sigmoid(gate_activation_values)
    grad_gate = (
        act_grad * up_vals * gate_sig * (1.0 + gate_activation_values * (1.0 - gate_sig))
    ).astype(jnp.bfloat16)
    up_projection_gradient = (act_grad * gate_activation_values * gate_sig).astype(jnp.bfloat16)
    activation = (gate_activation_values * gate_sig * up_vals).astype(jnp.bfloat16)
    partial_value_term = lax.dot_general(
        incoming,
        lax.all_gather(activation, "et", axis=0, tiled=True),
        (((0,), (1,)), ((), ())),
        preferred_element_type=jnp.float32,
    )
    summed = lax.psum_scatter(
        partial_value_term.astype(jnp.bfloat16), "rep", scatter_dimension=0, tiled=True
    )
    grad_down = summed[None]
    return (grad_gate[None, None], up_projection_gradient[None, None], grad_down)


def solution(mesh):
    return jax.shard_map(
        local,
        mesh=mesh,
        in_specs=(
            P(("ep", "rep"), "et"),
            P(("ep", "rep"), None),
            P(("ep", "rep"), None),
            P("ep", "et", None),
            P("ep", "rep", "et", None),
            P("ep", "rep", "et", None),
        ),
        out_specs=(
            P("ep", "rep", "et", None),
            P("ep", "rep", "et", None),
            P("ep", ("et", "rep"), None),
        ),
        check_vma=False,
    )
```

profile of v0, /device:TPU:0, one launch (start us, length us, event | category | flops | bytes accessed | tf_op | source)
XLA Modules:
  0.0 214.2 jit_solution(3642128905104083742)
XLA Ops:
  7.2 0.8 copy.20
  8.0 0.1 reshape.78
  8.3 1.2 reduce-window.6
  9.6 0.2 slice_reduce_fusion
  9.8 0.2 reduce-window.9
  10.1 0.2 fusion.5
  10.3 0.2 select_reduce_fusion
  10.8 0.8 copy.22
  11.7 3.9 %mul.58 = f32[256,2,1792]{2,1,0:T(2,128)} broadcast(bf16[256,1792]{1,0:T(8,128)(2,1)} %param.6), dimensions={0,2} | broadcast | bytes 4587520 | tf_op jit(solution)/shard_map/mul | solution.py:30
  15.6 5.6 %mul.59 = f32[512,1792]{1,0:T(8,128)} reshape(f32[256,2,1792]{2,1,0:T(2,128)} %mul.58) | data formatting | bytes 7340032 | tf_op jit(solution)/shard_map/mul | solution.py:30
  21.2 2.3 %multiply_convert_fusion = bf16[512,1792]{1,0:T(8,128)(2,1)S(1)} fusion(f32[512,1792]{1,0:T(8,128)} %mul.59, f32[512]{0:T(512)S(1)} %mul.60), kind=kLoop, calls=%fused_computation.4 | loop fusion | flops 1835008 | bytes 5507072 | tf_op jit(solution)/shard_map/convert_element_type | solution.py:32
  23.5 4.1 %gather_fusion = bf16[768,1792]{1,0:T(8,128)(2,1)} fusion(bf16[512,1792]{1,0:T(8,128)(2,1)S(1)} %multiply_convert_fusion, s32[1024]{0:T(1024)S(1)} %pad_clamp_fusion), kind=kCustom, calls=%fused_computation | custom fusion | bytes 5508096 | tf_op jit(solution)/shard_map/jit(_take)/gather | solution.py:35
  27.6 2.1 select_select_fusion
  29.6 68.6 %all_to_all.5 = bf16[4,192,1792]{2,1,0:T(8,128)(2,1)S(1)} all-to-all(bf16[4,192,1792]{2,1,0:T(8,128)(2,1)S(1)} %select_select_fusion), channel_id=1, replica_groups=mesh['ep'=4,'et'=4,'rep'=2] {'ep'}, dimensions={0} | all-to-all | bytes 5505024 | tf_op jit(solution)/shard_map/all_to_all | solution.py:38
  98.3 4.1 %fusion.6 = bf16[1024,768]{0,1:T(8,128)(2,1)} fusion(bf16[768,1792]{1,0:T(8,128)(2,1)S(1)} %bitcast.54, bf16[1,1792,1024]{2,1,0:T(8,128)(2,1)S(1)} %copy-done.2), kind=kOutput, calls=%fused_computation.10 | convolution fusion | flops 2819358720 | bytes 7995392 | tf_op jit(solution)/shard_map/dot_general | solution.py:43
  102.5 0.9 copy.24
  103.4 0.9 copy.23
  104.3 25.7 %reduce-scatter.3.cloned.1.call-done = bf16[256,768]{0,1:T(8,128)(2,1)} async-done(((bf16[1024,768]{0,1:T(8,128)(2,1)}), bf16[256,768]{0,1:T(8,128)(2,1)}) %reduce-scatter.3.cloned.1.call-update) | async-done | bytes 393232 | tf_op jit(solution)/shard_map/reduce_scatter | solution.py:42
  130.0 2.5 %fusion.12 = (bf16[256,768]{0,1:T(8,128)(2,1)}, bf16[1,1,256,768]{2,3,1,0:T(8,128)(2,1)S(1)}, bf16[1,1,256,768]{2,3,1,0:T(8,128)(2,1)S(1)}) fusion(bf16[1,1,256,768]{2,3,1,0:T(8,128)(2,1)} %copy.23, bf16[1,1,256,768]{2,3,1,0:T(8,128)(2,1)} %copy.24, bf16[256,768]{0,1:T(8,128)(2,1)} %reduce-scatter.3.cloned.1.call-done), kind=kLoop, calls=%fused_computation.20 | loop fusion | flops 3735552 | bytes 2359296 | tf_op jit(solution)/shard_map/convert_element_type | solution.py:57
  132.5 20.0 %all-gather.2.cloned.1.call-done = bf16[1024,768]{0,1:T(8,128)(2,1)} async-done(((bf16[256,768]{0,1:T(8,128)(2,1)}), bf16[1024,768]{0,1:T(8,128)(2,1)}) %all-gather.2.cloned.1.call-update) | async-done | bytes 1572880 | tf_op jit(solution)/shard_map/all_gather | solution.py:60
  152.5 5.9 %convolution_convert_fusion = bf16[1792,1024]{1,0:T(8,128)(2,1)} fusion(bf16[768,1792]{1,0:T(8,128)(2,1)S(1)} %bitcast.55, bf16[1024,768]{0,1:T(8,128)(2,1)} %all-gather.2.cloned.1.call-done), kind=kOutput, calls=%fused_computation.1 | convolution fusion | flops 2820407296 | bytes 7995392 | tf_op jit(solution)/shard_map/dot_general | solution.py:58
  158.4 0.9 copy.25
  159.3 0.9 copy.26
  160.3 47.4 %reduce-scatter.5.cloned.1.call-done = bf16[896,1024]{1,0:T(8,128)(2,1)} async-done(((bf16[1792,1024]{1,0:T(8,128)(2,1)}), bf16[896,1024]{1,0:T(8,128)(2,1)}) %reduce-scatter.5.cloned.1.call-update) | async-done | bytes 1835024 | tf_op jit(solution)/shard_map/reduce_scatter | solution.py:64
  (23 shorter events, 0.8 us)
Async XLA Ops:
  7.2 122.8 %reduce-scatter.3.cloned.1.call-start = ((), (), s32[]{:S(2)}) async-start(), calls=%async_computation.3 | async-start | bytes 1966080 | tf_op jit(solution)/shard_map/reduce_scatter | solution.py:42
  29.6 68.6 %copy-start.2 = (bf16[1,1792,1024]{2,1,0:T(8,128)(2,1)S(1)}, bf16[1,1792,1024]{2,1,0:T(8,128)(2,1)}, u32[]{:S(2)}) copy-start(bf16[1,1792,1024]{2,1,0:T(8,128)(2,1)} %param.9) | copy-start | bytes 11010052
  98.3 4.2 %copy-start = (bf16[1,1,256,768]{3,2,1,0:T(8,128)(2,1)S(1)}, bf16[1,1,256,768]{3,2,1,0:T(8,128)(2,1)}, u32[]{:S(2)}) copy-start(bf16[1,1,256,768]{3,2,1,0:T(8,128)(2,1)} %param.10) | copy-start | bytes 1179652
  98.3 5.1 %copy-start.1 = (bf16[1,1,256,768]{3,2,1,0:T(8,128)(2,1)S(1)}, bf16[1,1,256,768]{3,2,1,0:T(8,128)(2,1)}, u32[]{:S(2)}) copy-start(bf16[1,1,256,768]{3,2,1,0:T(8,128)(2,1)} %param.11) | copy-start | bytes 1179652
  102.4 50.1 %all-gather.2.cloned.1.call-start = ((), (), s32[]{:S(2)}) async-start(), calls=%async_computation.4 | async-start | bytes 1966080 | tf_op jit(solution)/shard_map/all_gather | solution.py:60
  132.5 75.2 %reduce-scatter.5.cloned.1.call-start = ((), (), s32[]{:S(2)}) async-start(), calls=%async_computation.5 | async-start | bytes 5505024 | tf_op jit(solution)/shard_map/reduce_scatter | solution.py:64
Sparse Core Ops, SparseCore 0:
  102.5 27.4 reduce-scatter.2
  132.6 19.8 all-gather.1
  158.5 49.0 reduce-scatter.4
where the time goes:
time: 215 us; the launch traced here: 214 us
  waiting for transfers between devices  93.1 us (43%)
  blocking collectives  68.6 us (32%)
  local copies, waits for them, and re-layouts  19.7 us (9%)
  between operations  13.8 us (6%)
  matrix products  10 us (5%)
  other arithmetic  8.85 us (4%)
    all_to_all x1, blocking collectives, local(): lax.all_to_all(outgoing, 'ep', split_axis=0, concat_axis=0, tiled=True)  68.6 us
    reduce_scatter x1, waiting for transfers between devices, local(): lax.psum_scatter(partial_value_term.astype(jnp.bfloat16), 'rep', scatter_...  47.4 us
    reduce_scatter x1, waiting for transfers between devices, local(): lax.psum_scatter(lax.dot_general(weight_rows, incoming, (((0,), (1,)), ((...  25.7 us
    all_gather x1, waiting for transfers between devices, local(): lax.all_gather(activation, 'et', axis=0, tiled=True)  20 us
    mul x3, local copies, waits for them, and re-layouts, local(): grad_out.astype(jnp.float32)[:, None, :] * combine[:, :, None]  9.64 us
    dot_general x1, matrix products, local(): lax.dot_general(incoming, lax.all_gather(activation, 'et', axis=0, tiled=...  5.92 us
    unnamed x12, local copies, waits for them, and re-layouts  5.31 us
  transfers between devices with their start and end apart: 3, of which 3 were waited for; matrix products, arithmetic and copies ran while one was open for 2% of the time, Pallas kernels for 0%

commit v1 on v0

v1 whole, which is shorter than its diff:
```python
import functools

import jax
import jax.numpy as jnp
from jax import lax
from jax.experimental import pallas as pl
from jax.experimental.pallas import tpu as pltpu
from jax.sharding import PartitionSpec as P

MESH = pl.DeviceIdType.MESH
F32 = jnp.float32
BF16 = jnp.bfloat16
AHEAD = (2, 1, 3)


def kernel(
    n_ep, n_et, grad_ref, comb_ref, route_ref, down_ref, gate_ref, up_ref,
    gg_ref, ug_ref, gd_ref,
    out_buf, in_buf, y_buf, weight, act_buf, part_buf, sum_buf, total, coef_g, coef_u, act_grad,
    key_buf, share_buf,
    w_sem, z_send, z_recv, y_send, y_recv, a_send, a_recv, p_send, p_recv,
):
    ep, et, rep = lax.axis_index("ep"), lax.axis_index("et"), lax.axis_index("rep")
    other = 1 - rep
    cap = in_buf.shape[2]
    hidden = gate_ref.shape[0]
    half = in_buf.shape[3]
    across = lax.rem(et + 2, n_et)
    beside = et + 1 - 2 * lax.rem(et, 2)

    def load_w(t):
        return pltpu.make_async_copy(
            down_ref.at[:, pl.ds(t * hidden, hidden)], weight.at[t], w_sem.at[t]
        )

    for t in range(n_et):
        load_w(t).start()

    barrier = pltpu.get_barrier_semaphore()
    for k in range(1, n_ep):
        pl.semaphore_signal(
            barrier, inc=1, device_id={"ep": lax.rem(ep + k, n_ep)}, device_id_type=MESH
        )
    for k in range(1, n_et):
        pl.semaphore_signal(
            barrier, inc=1, device_id={"et": lax.rem(et + k, n_et)}, device_id_type=MESH
        )
    pl.semaphore_signal(barrier, inc=1, device_id={"rep": other}, device_id_type=MESH)

    tokens = grad_ref.shape[0]
    rows = key_buf.shape[0]
    names = lax.broadcasted_iota(jnp.int32, (rows, tokens), 0)
    first = route_ref[0:1, :] == names
    mine = first | (route_ref[1:2, :] == names)
    before = (
        lax.broadcasted_iota(jnp.int32, (tokens, tokens), 0)
        < lax.broadcasted_iota(jnp.int32, (tokens, tokens), 1)
    )
    rank = jnp.dot(
        jnp.where(mine, 1.0, 0.0).astype(BF16),
        jnp.where(before, 1.0, 0.0).astype(BF16),
        preferred_element_type=F32,
    )
    key_buf[...] = jnp.where(mine, rank, -1.0)
    share_buf[...] = jnp.where(first, comb_ref[0:1, :], comb_ref[1:2, :])
    places = lax.broadcasted_iota(jnp.int32, (cap, tokens), 0).astype(F32)

    def pick(expert):
        chosen = key_buf[pl.ds(expert, 1), :] == places
        scale = jnp.sum(
            jnp.where(chosen, share_buf[pl.ds(expert, 1), :], 0.0), axis=1, keepdims=True
        )
        return jnp.where(chosen, 1.0, 0.0).astype(BF16), scale

    def routed(pick_of, h):
        chosen, scale = pick_of
        columns = grad_ref[:, pl.ds(pl.multiple_of(h * half, 128), half)]
        return (jnp.dot(chosen, columns, preferred_element_type=F32) * scale).astype(BF16)

    def z_copy(h, expert, source):
        return pltpu.make_async_remote_copy(
            src_ref=out_buf.at[h, expert],
            dst_ref=in_buf.at[h, source],
            send_sem=z_send.at[h, expert],
            recv_sem=z_recv.at[h, source],
            device_id={"ep": expert},
            device_id_type=MESH,
        )

    def y_copy(h, source):
        return pltpu.make_async_remote_copy(
            src_ref=in_buf.at[h, source],
            dst_ref=y_buf.at[source],
            send_sem=y_send.at[source],
            recv_sem=y_recv.at[source],
            device_id={"rep": other},
            device_id_type=MESH,
        )

    def a_copy(i, r, t, target):
        return pltpu.make_async_remote_copy(
            src_ref=act_buf.at[r, t],
            dst_ref=act_buf.at[r, t],
            send_sem=a_send.at[i],
            recv_sem=a_recv.at[i],
            device_id=target,
            device_id_type=MESH,
        )

    def p_copy(source, t, sender):
        return pltpu.make_async_remote_copy(
            src_ref=part_buf.at[source, t],
            dst_ref=sum_buf.at[source, sender],
            send_sem=p_send.at[source, t],
            recv_sem=p_recv.at[source, sender],
            device_id={"et": t},
            device_id_type=MESH,
        )

    for n, k in enumerate(AHEAD):
        expert = lax.rem(ep + k, n_ep)
        chosen = pick(expert)
        for h in (other, rep):
            out_buf[h, expert] = routed(chosen, h)
        if n == 0:
            pl.semaphore_wait(barrier, n_ep - 1 + n_et - 1 + 1)
        for h in (other, rep):
            z_copy(h, expert, ep).start()
    chosen = pick(ep)
    for h in (other, rep):
        in_buf[h, ep] = routed(chosen, h)
    y_copy(other, ep).start()

    h_value, u_value = gate_ref[...].astype(F32), up_ref[...].astype(F32)
    sig = 1.0 / (1.0 + jnp.exp(-h_value))
    silu = h_value * sig
    coef_g[...] = u_value * sig * (1.0 + h_value * (1.0 - sig))
    coef_u[...] = silu
    act_buf[rep, et] = (silu * u_value).T.astype(BF16)
    to_y, to_x, to_c = {"rep": other}, {"et": across}, {"et": beside}
    a_copy(0, rep, et, to_y).start()
    a_copy(1, rep, et, to_x).start()
    a_copy(3, rep, et, to_c).start()

    for t in range(n_et):
        load_w(t).wait()

    def partial(source):
        def one(k, carry):
            t = lax.rem(et + k, n_et)
            value = jnp.dot(
                in_buf[0, source], weight[t, pl.ds(0, half)], preferred_element_type=F32
            ) + jnp.dot(
                in_buf[1, source], weight[t, pl.ds(half, half)], preferred_element_type=F32
            )
            part_buf[source, t] = value.astype(BF16)

            @pl.when(k < n_et)
            def _():
                p_copy(source, t, et).start()

            return carry

        lax.fori_loop(1, n_et + 1, one, 0)

    def weigh(slots_ref, r, source, start=False):
        turned = slots_ref[...].T
        at = pl.multiple_of(source * cap, 16)
        for t in range(n_et):
            value = jnp.dot(
                turned, act_buf[r, t, pl.ds(at, cap), :], preferred_element_type=F32
            )
            total[t] = value if start else total[t] + value

    partial(ep)
    a_copy(0, other, et, to_y).wait_recv()
    a_copy(2, other, et, to_x).start()
    a_copy(4, other, et, to_c).start()
    a_copy(1, rep, across, to_x).wait_recv()
    a_copy(5, rep, across, to_c).start()
    a_copy(2, other, across, to_x).wait_recv()
    a_copy(6, other, across, to_c).start()
    far = lax.rem(beside + 2, n_et)
    a_copy(3, rep, beside, to_c).wait_recv()
    a_copy(4, other, beside, to_c).wait_recv()
    a_copy(5, rep, far, to_c).wait_recv()
    a_copy(6, other, far, to_c).wait_recv()
    weigh(in_buf.at[rep, ep], rep, ep, True)
    y_copy(other, ep).wait_recv()
    weigh(y_buf.at[ep], other, ep)

    def gather(source):
        value = part_buf[source, et].astype(F32)
        for k in range(1, n_et):
            sender = lax.rem(et + k, n_et)
            p_copy(source, et, sender).wait_recv()
            value = value + sum_buf[source, sender].astype(F32)
        act_grad[pl.ds(pl.multiple_of(source * cap, 16), cap), :] = value

    earlier = ep
    for k in AHEAD:
        source = lax.rem(ep + n_ep - k, n_ep)
        z_copy(other, ep, source).wait_recv()
        y_copy(other, source).start()
        z_copy(rep, ep, source).wait_recv()
        partial(source)
        weigh(in_buf.at[rep, source], rep, source)
        if k != AHEAD[0]:
            y_copy(other, earlier).wait_recv()
            weigh(y_buf.at[earlier], other, earlier)
        gather(earlier)
        earlier = source
    gather(earlier)
    value = act_grad[...].T
    gg_ref[...] = (value * coef_g[...]).astype(BF16)
    ug_ref[...] = (value * coef_u[...]).astype(BF16)
    y_copy(other, earlier).wait_recv()
    weigh(y_buf.at[earlier], other, earlier)
    for t in range(n_et):
        gd_ref[:, pl.ds(t * hidden, hidden)] = total[t].astype(BF16)

    for i, (r, t, target) in enumerate((
        (rep, et, to_y), (rep, et, to_x), (other, et, to_x),
        (rep, et, to_c), (other, et, to_c), (rep, across, to_c), (other, across, to_c),
    )):
        a_copy(i, r, t, target).wait_send()
    for k in range(n_ep):
        source = lax.rem(ep + k, n_ep)
        y_copy(other, source).wait_send()
        if k > 0:
            z_copy(other, source, ep).wait_send()
            z_copy(rep, source, ep).wait_send()
        for j in range(1, n_et):
            p_copy(source, lax.rem(et + j, n_et), et).wait_send()


def fused(n_ep, n_et, grad_out, combine, routing, expert_down_matrix, gate_pre, up_pre):
    tokens, feats = grad_out.shape
    hidden, slots = gate_pre.shape[2:]
    cap, half = slots // n_ep, feats // 2
    vmem = pl.BlockSpec(memory_space=pltpu.VMEM)
    dma = pltpu.SemaphoreType.DMA
    gg, ug, gd = pl.pallas_call(
        functools.partial(kernel, n_ep, n_et),
        out_shape=(
            jax.ShapeDtypeStruct((hidden, slots), BF16),
            jax.ShapeDtypeStruct((hidden, slots), BF16),
            jax.ShapeDtypeStruct((half, n_et * hidden), BF16),
        ),
        in_specs=[vmem, vmem, vmem, pl.BlockSpec(memory_space=pl.ANY), vmem, vmem],
        out_specs=(vmem, vmem, vmem),
        scratch_shapes=[
            pltpu.VMEM((2, n_ep, cap, half), BF16),
            pltpu.VMEM((2, n_ep, cap, half), BF16),
            pltpu.VMEM((n_ep, cap, half), BF16),
            pltpu.VMEM((n_et, feats, hidden), BF16),
            pltpu.VMEM((2, n_et, slots, hidden), BF16),
            pltpu.VMEM((n_ep, n_et, cap, hidden), BF16),
            pltpu.VMEM((n_ep, n_et, cap, hidden), BF16),
            pltpu.VMEM((n_et, half, hidden), F32),
            pltpu.VMEM((hidden, slots), F32),
            pltpu.VMEM((hidden, slots), F32),
            pltpu.VMEM((slots, hidden), F32),
            pltpu.VMEM((16, tokens), F32),
            pltpu.VMEM((16, tokens), F32),
            dma((n_et,)),
            dma((2, n_ep)),
            dma((2, n_ep)),
            dma((n_ep,)),
            dma((n_ep,)),
            dma((7,)),
            dma((7,)),
            dma((n_ep, n_et)),
            dma((n_ep, n_et)),
        ],
        compiler_params=pltpu.CompilerParams(
            collective_id=0, has_side_effects=True, vmem_limit_bytes=50 * 2**20
        ),
    )(grad_out, combine.T, routing.T, expert_down_matrix[0], gate_pre[0, 0], up_pre[0, 0])
    return gg[None, None], ug[None, None], gd[None]


def plain(n_ep, grad_out, combine, routing, expert_down_matrix, gate_pre, up_pre):
    slot_count = gate_pre.shape[-1]
    cap = slot_count // n_ep
    tokens, feats = grad_out.shape
    width = routing.shape[1]
    pairs = tokens * width
    targets = routing.reshape(pairs)
    onehot = targets[:, None] == jnp.arange(n_ep, dtype=jnp.int32)[None, :]
    place = jnp.arange(pairs, dtype=jnp.int32)
    before = (place[None, :] < place[:, None]).astype(BF16)
    counts = jnp.dot(before, onehot.astype(BF16), preferred_element_type=F32)
    ranking = jnp.sum(jnp.where(onehot, counts, 0.0), axis=1).astype(jnp.int32)
    destination = targets * cap + ranking
    matches = destination[None, :] == jnp.arange(slot_count, dtype=jnp.int32)[:, None]
    filled = jnp.any(matches, axis=1)
    source = jnp.sum(jnp.where(matches, place[None, :], 0), axis=1, dtype=jnp.int32)
    scale = jnp.take(combine.reshape(pairs), source)
    rows = jnp.take(grad_out, source // width, axis=0).astype(F32)
    outgoing = jnp.where(filled[:, None], (rows * scale[:, None]).astype(BF16), jnp.zeros((), BF16))
    incoming = lax.all_to_all(
        outgoing.reshape(n_ep, cap, feats), "ep", split_axis=0, concat_axis=0, tiled=True
    ).reshape(slot_count, feats)
    act_grad = lax.psum_scatter(
        lax.dot_general(
            expert_down_matrix[0], incoming, (((0,), (1,)), ((), ())), preferred_element_type=F32
        ).astype(BF16),
        "et",
        scatter_dimension=0,
        tiled=True,
    ).astype(F32)
    h, u = gate_pre[0, 0].astype(F32), up_pre[0, 0].astype(F32)
    sig = jax.nn.sigmoid(h)
    grad_gate = (act_grad * u * sig * (1.0 + h * (1.0 - sig))).astype(BF16)
    up_grad = (act_grad * h * sig).astype(BF16)
    activation = (h * sig * u).astype(BF16)
    part = lax.dot_general(
        incoming,
        lax.all_gather(activation, "et", axis=0, tiled=True),
        (((0,), (1,)), ((), ())),
        preferred_element_type=F32,
    ).astype(BF16)
    grad_down = lax.psum_scatter(part, "rep", scatter_dimension=0, tiled=True)
    return grad_gate[None, None], up_grad[None, None], grad_down[None]


def solution(mesh):
    n_ep, n_et, n_rep = mesh.shape["ep"], mesh.shape["et"], mesh.shape["rep"]

    def local(grad_out, combine, routing, expert_down_matrix, gate_pre, up_pre):
        args = (grad_out, combine, routing, expert_down_matrix, gate_pre, up_pre)
        whole_tiles = gate_pre.shape[-1] // n_ep % 16 == 0
        if n_ep == 4 and n_et == 4 and n_rep == 2 and whole_tiles:
            return fused(n_ep, n_et, *args)
        return plain(n_ep, *args)

    return jax.shard_map(
        local,
        mesh=mesh,
        in_specs=(
            P(("ep", "rep"), "et"),
            P(("ep", "rep"), None),
            P(("ep", "rep"), None),
            P("ep", "et", None),
            P("ep", "rep", "et", None),
            P("ep", "rep", "et", None),
        ),
        out_specs=(
            P("ep", "rep", "et", None),
            P("ep", "rep", "et", None),
            P("ep", ("et", "rep"), None),
        ),
        check_vma=False,
    )
```

time: 215 us -> 86.5 us (0.40)
  the two profiles are of different devices: /device:TPU:0 before, /device:TPU:16 now
where the time goes in v1:
time: 86.5 us; the launch traced here: 86.2 us
  Pallas kernels  76.7 us (89%)
  local copies, waits for them, and re-layouts  8.89 us (10%)
    pallas_call x1, Pallas kernels, fused(): pl.pallas_call(functools.partial(kernel, n_ep, n_et), out_shape=(jax.Shap...  76.7 us
    unnamed x13, local copies, waits for them, and re-layouts  8.89 us

profile of v1, /device:TPU:16, one launch (start us, length us, event | category | flops | bytes accessed | tf_op | source)
XLA Modules:
  0.0 86.2 jit_solution(5715484290190500941)
XLA Ops:
  0.6 0.0 copy-start
  0.6 1.2 %copy-done = bf16[256,1792]{1,0:T(8,128)(2,1)S(1)} copy-done((bf16[256,1792]{1,0:T(8,128)(2,1)S(1)}, bf16[256,1792]{1,0:T(8,128)(2,1)}, u32[]{:S(2)}) %copy-start) | copy-done | bytes 917528
  1.8 0.0 copy-start.1
  1.8 1.0 %copy-done.1 = bf16[1,1,256,768]{3,2,1,0:T(8,128)(2,1)S(1)} copy-done((bf16[1,1,256,768]{3,2,1,0:T(8,128)(2,1)S(1)}, bf16[1,1,256,768]{3,2,1,0:T(8,128)(2,1)}, u32[]{:S(2)}) %copy-start.1) | copy-done | bytes 393240
  2.8 0.0 copy-start.2
  2.8 1.0 %copy-done.2 = bf16[1,1,256,768]{3,2,1,0:T(8,128)(2,1)S(1)} copy-done((bf16[1,1,256,768]{3,2,1,0:T(8,128)(2,1)S(1)}, bf16[1,1,256,768]{3,2,1,0:T(8,128)(2,1)}, u32[]{:S(2)}) %copy-start.2) | copy-done | bytes 393240
  3.8 0.0 copy-start.3
  3.8 0.7 copy-done.3
  4.5 0.0 copy-start.4
  4.5 0.7 copy-done.4
  5.2 76.7 %shard_map.85 = (bf16[256,768]{1,0:T(8,128)(2,1)S(1)}, bf16[256,768]{1,0:T(8,128)(2,1)S(1)}, bf16[896,1024]{1,0:T(8,128)(2,1)}) custom-call(bf16[256,1792]{1,0:T(8,128)(2,1)S(1)} %copy-done, f32[2,256]{1,0:T(2,128)S(1)} %bitcast.12, s32[2,256]{1,0:T(2,128)S(1)} %bitcast.13, bf16[1792,1024]{1,0:T(8,128)(2,1)} %bitcast.14, bf16[256,768]{1,0:T(8,128)(2,1)S(1)} %bitcast.8, ...), custom_call_target="tpu_custom_call" | custom-call | tf_op jit(solution)/shard_map/pallas_call | solution.py:243
  81.8 0.7 copy.12
  82.6 0.7 copy.13
  83.3 2.9 %copy.14 = bf16[1,896,1024]{2,1,0:T(8,128)(2,1)} copy(bf16[1,896,1024]{2,1,0:T(8,128)(2,1)} %bitcast.15) | data formatting | bytes 3670016
Async XLA Ops:
  0.6 1.2 %copy-start = (bf16[256,1792]{1,0:T(8,128)(2,1)S(1)}, bf16[256,1792]{1,0:T(8,128)(2,1)}, u32[]{:S(2)}) copy-start(bf16[256,1792]{1,0:T(8,128)(2,1)} %grad_ref.1) | copy-start | bytes 2752516
  1.8 1.0 %copy-start.1 = (bf16[1,1,256,768]{3,2,1,0:T(8,128)(2,1)S(1)}, bf16[1,1,256,768]{3,2,1,0:T(8,128)(2,1)}, u32[]{:S(2)}) copy-start(bf16[1,1,256,768]{3,2,1,0:T(8,128)(2,1)} %param.10) | copy-start | bytes 1179652
  2.8 1.0 %copy-start.2 = (bf16[1,1,256,768]{3,2,1,0:T(8,128)(2,1)S(1)}, bf16[1,1,256,768]{3,2,1,0:T(8,128)(2,1)}, u32[]{:S(2)}) copy-start(bf16[1,1,256,768]{3,2,1,0:T(8,128)(2,1)} %param.11) | copy-start | bytes 1179652
  3.8 0.7 copy-start.3
  4.5 0.7 copy-start.4

commit v2 on v1

v2 whole, which is shorter than its diff:
```python
import functools

import jax
import jax.numpy as jnp
from jax import lax
from jax.experimental import pallas as pl
from jax.experimental.pallas import tpu as pltpu
from jax.sharding import PartitionSpec as P

MESH = pl.DeviceIdType.MESH
F32 = jnp.float32
BF16 = jnp.bfloat16


def kernel(
    n_ep, n_et, grad_hbm, comb_hbm, route_hbm, down_ref, gate_hbm, up_hbm,
    gg_ref, ug_ref, gd_ref,
    tok_buf, meta_buf, out_buf, in_buf, y_buf, weight, act_buf, part_buf, sum_buf, total,
    coef_g, coef_u, act_grad, comb_ref, route_ref, gate_ref, up_ref,
    w_sem, l_sem, t_send, t_recv, m_send, m_recv,
    z_send, z_recv, y_send, y_recv, a_send, a_recv, p_send, p_recv,
):
    ep, et, rep = lax.axis_index("ep"), lax.axis_index("et"), lax.axis_index("rep")
    other = 1 - rep
    cap, half = in_buf.shape[2:]
    tokens = tok_buf.shape[2]
    hidden = gate_ref.shape[0]
    across = lax.rem(et + 2, n_et)
    beside = et + 1 - 2 * lax.rem(et, 2)
    last = n_ep - 1
    near = ep + 1 - 2 * lax.rem(ep, 2)
    inner = lax.rem((ep + 1) // 2, 2)
    is_inner = inner == 1
    second = inner * (last - ep) + (1 - inner) * (last - near)
    third = inner * (last - near) + (1 - inner) * (last - ep)
    onward = inner * (last - ep) + (1 - inner) * near

    def load(i):
        if i < 2:
            h = (other, rep)[i]
            columns = pl.ds(pl.multiple_of(h * half, 128), half)
            return pltpu.make_async_copy(grad_hbm.at[:, columns], tok_buf.at[ep, h], l_sem.at[i])
        source, target = (
            (comb_hbm, comb_ref), (route_hbm, route_ref), (gate_hbm, gate_ref), (up_hbm, up_ref)
        )[i - 2]
        return pltpu.make_async_copy(source, target, l_sem.at[i])

    def load_w(t):
        return pltpu.make_async_copy(
            down_ref.at[:, pl.ds(t * hidden, hidden)], weight.at[t], w_sem.at[t]
        )

    barrier = pltpu.get_barrier_semaphore()
    for k in range(1, n_ep):
        pl.semaphore_signal(
            barrier, inc=1, device_id={"ep": lax.rem(ep + k, n_ep)}, device_id_type=MESH
        )
    for k in range(1, n_et):
        pl.semaphore_signal(
            barrier, inc=1, device_id={"et": lax.rem(et + k, n_et)}, device_id_type=MESH
        )
    pl.semaphore_signal(barrier, inc=1, device_id={"rep": other}, device_id_type=MESH)
    for i in (2, 3, 0, 1, 4, 5):
        load(i).start()
    for t in range(n_et):
        load_w(t).start()

    def t_copy(source, h):
        return pltpu.make_async_remote_copy(
            src_ref=tok_buf.at[source, h],
            dst_ref=tok_buf.at[source, h],
            send_sem=t_send.at[source, h],
            recv_sem=t_recv.at[source, h],
            device_id={"ep": onward},
            device_id_type=MESH,
        )

    def m_copy(source):
        return pltpu.make_async_remote_copy(
            src_ref=meta_buf.at[source],
            dst_ref=meta_buf.at[source],
            send_sem=m_send.at[source],
            recv_sem=m_recv.at[source],
            device_id={"ep": onward},
            device_id_type=MESH,
        )

    def z_copy(source, h):
        return pltpu.make_async_remote_copy(
            src_ref=out_buf.at[h, source],
            dst_ref=in_buf.at[h, source],
            send_sem=z_send.at[h, source],
            recv_sem=z_recv.at[h, source],
            device_id={"ep": near},
            device_id_type=MESH,
        )

    def y_copy(source):
        return pltpu.make_async_remote_copy(
            src_ref=in_buf.at[other, source],
            dst_ref=y_buf.at[source],
            send_sem=y_send.at[source],
            recv_sem=y_recv.at[source],
            device_id={"rep": other},
            device_id_type=MESH,
        )

    def a_copy(i, r, t, target):
        return pltpu.make_async_remote_copy(
            src_ref=act_buf.at[r, t],
            dst_ref=act_buf.at[r, t],
            send_sem=a_send.at[i],
            recv_sem=a_recv.at[i],
            device_id=target,
            device_id_type=MESH,
        )

    def p_copy(source, t, sender):
        return pltpu.make_async_remote_copy(
            src_ref=part_buf.at[source, t],
            dst_ref=sum_buf.at[source, sender],
            send_sem=p_send.at[source, t],
            recv_sem=p_recv.at[source, sender],
            device_id={"et": t},
            device_id_type=MESH,
        )

    load(2).wait()
    load(3).wait()
    rows = meta_buf.shape[2]
    names = lax.broadcasted_iota(jnp.int32, (rows, tokens), 0)
    first = route_ref[0:1, :] == names
    mine = first | (route_ref[1:2, :] == names)
    before = (
        lax.broadcasted_iota(jnp.int32, (tokens, tokens), 0)
        < lax.broadcasted_iota(jnp.int32, (tokens, tokens), 1)
    )
    rank = jnp.dot(
        jnp.where(mine, 1.0, 0.0).astype(BF16),
        jnp.where(before, 1.0, 0.0).astype(BF16),
        preferred_element_type=F32,
    )
    meta_buf[ep, 0] = jnp.where(mine, rank, -1.0)
    meta_buf[ep, 1] = jnp.where(first, comb_ref[0:1, :], comb_ref[1:2, :])
    places = lax.broadcasted_iota(jnp.int32, (cap, tokens), 0).astype(F32)

    def routed(source, h, expert):
        chosen = meta_buf[source, 0, pl.ds(expert, 1), :] == places
        scale = jnp.sum(
            jnp.where(chosen, meta_buf[source, 1, pl.ds(expert, 1), :], 0.0),
            axis=1,
            keepdims=True,
        )
        picked = jnp.dot(
            jnp.where(chosen, 1.0, 0.0).astype(BF16),
            tok_buf[source, h],
            preferred_element_type=F32,
        )
        return (picked * scale).astype(BF16)

    pl.semaphore_wait(barrier, n_ep - 1 + n_et - 1 + 1)
    m_copy(ep).start()
    for i, h in enumerate((other, rep)):
        load(i).wait()
        t_copy(ep, h).start()

    def pass_slots(source, h):
        out_buf[h, source] = routed(source, h, near)
        z_copy(source, h).start()

    @pl.when(is_inner)
    def _():
        for h in (other, rep):
            pass_slots(ep, h)

    in_buf[other, ep] = routed(ep, other, ep)
    y_copy(ep).start()
    in_buf[rep, ep] = routed(ep, rep, ep)

    load(4).wait()
    load(5).wait()
    h_value, u_value = gate_ref[...].astype(F32), up_ref[...].astype(F32)
    sig = 1.0 / (1.0 + jnp.exp(-h_value))
    silu = h_value * sig
    act_buf[rep, et] = (silu * u_value).T.astype(BF16)
    to_y, to_x, to_c = {"rep": other}, {"et": across}, {"et": beside}
    a_copy(0, rep, et, to_y).start()
    a_copy(1, rep, et, to_x).start()
    a_copy(3, rep, et, to_c).start()
    coef_g[...] = u_value * sig * (1.0 + h_value * (1.0 - sig))
    coef_u[...] = silu

    def partial(source):
        def one(k, carry):
            t = lax.rem(et + k, n_et)
            value = jnp.dot(
                in_buf[0, source], weight[t, pl.ds(0, half)], preferred_element_type=F32
            ) + jnp.dot(
                in_buf[1, source], weight[t, pl.ds(half, half)], preferred_element_type=F32
            )
            part_buf[source, t] = value.astype(BF16)

            @pl.when(k < n_et)
            def _():
                p_copy(source, t, et).start()

            return carry

        lax.fori_loop(1, n_et + 1, one, 0)

    def weigh(slots_ref, r, source, start=False):
        turned = slots_ref[...].T
        at = pl.multiple_of(source * cap, 16)
        for t in range(n_et):
            value = jnp.dot(
                turned, act_buf[r, t, pl.ds(at, cap), :], preferred_element_type=F32
            )
            total[t] = value if start else total[t] + value

    def weigh_own(source, start=False):
        weigh(in_buf.at[rep, source], rep, source, start)

    def weigh_y(source):
        y_copy(source).wait_recv()
        weigh(y_buf.at[source], other, source)

    def gather(source):
        value = part_buf[source, et].astype(F32)
        for k in range(1, n_et):
            sender = lax.rem(et + k, n_et)
            p_copy(source, et, sender).wait_recv()
            value = value + sum_buf[source, sender].astype(F32)
        act_grad[pl.ds(pl.multiple_of(source * cap, 16), cap), :] = value

    def arrive(which, h):
        source = (near, second, third)[which]

        @pl.when(is_inner)
        def _():
            if h is other:
                m_copy(source).wait_recv()
            t_copy(source, h).wait_recv()
            if which == 0:
                if h is other:
                    m_copy(source).start()
                t_copy(source, h).start()
            else:
                pass_slots(source, h)
            in_buf[h, source] = routed(source, h, ep)

        @pl.when(inner == 0)
        def _():
            z_copy(source, h).wait_recv()

        if h is other:
            y_copy(source).start()

    for t in range(n_et):
        load_w(t).wait()
    partial(ep)
    arrive(0, other)
    a_copy(0, other, et, to_y).wait_recv()
    a_copy(2, other, et, to_x).start()
    a_copy(4, other, et, to_c).start()
    a_copy(1, rep, across, to_x).wait_recv()
    a_copy(5, rep, across, to_c).start()
    arrive(1, other)
    gather(ep)
    arrive(0, rep)
    a_copy(2, other, across, to_x).wait_recv()
    a_copy(6, other, across, to_c).start()
    partial(near)
    arrive(1, rep)
    partial(second)
    far = lax.rem(beside + 2, n_et)
    a_copy(3, rep, beside, to_c).wait_recv()
    a_copy(4, other, beside, to_c).wait_recv()
    a_copy(5, rep, far, to_c).wait_recv()
    a_copy(6, other, far, to_c).wait_recv()
    weigh_own(ep, True)
    weigh_y(ep)
    weigh_own(near)
    gather(near)
    arrive(2, other)
    weigh_y(near)
    weigh_own(second)
    gather(second)
    arrive(2, rep)
    partial(third)
    weigh_y(second)
    weigh_own(third)
    weigh_y(third)
    for t in range(n_et):
        gd_ref[:, pl.ds(t * hidden, hidden)] = total[t].astype(BF16)
    gather(third)
    value = act_grad[...].T
    gg_ref[...] = (value * coef_g[...]).astype(BF16)
    ug_ref[...] = (value * coef_u[...]).astype(BF16)

    for i, (r, t, target) in enumerate((
        (rep, et, to_y), (rep, et, to_x), (other, et, to_x),
        (rep, et, to_c), (other, et, to_c), (rep, across, to_c), (other, across, to_c),
    )):
        a_copy(i, r, t, target).wait_send()
    m_copy(ep).wait_send()
    for h in (other, rep):
        t_copy(ep, h).wait_send()

    @pl.when(is_inner)
    def _():
        m_copy(near).wait_send()
        for h in (other, rep):
            t_copy(near, h).wait_send()
            for source in (ep, second, third):
                z_copy(source, h).wait_send()

    for source in (ep, near, second, third):
        y_copy(source).wait_send()
        for j in range(1, n_et):
            p_copy(source, lax.rem(et + j, n_et), et).wait_send()


def fused(n_ep, n_et, grad_out, combine, routing, expert_down_matrix, gate_pre, up_pre):
    tokens, feats = grad_out.shape
    hidden, slots = gate_pre.shape[2:]
    cap, half = slots // n_ep, feats // 2
    width = routing.shape[1]
    vmem = pl.BlockSpec(memory_space=pltpu.VMEM)
    dma = pltpu.SemaphoreType.DMA
    gg, ug, gd = pl.pallas_call(
        functools.partial(kernel, n_ep, n_et),
        out_shape=(
            jax.ShapeDtypeStruct((hidden, slots), BF16),
            jax.ShapeDtypeStruct((hidden, slots), BF16),
            jax.ShapeDtypeStruct((half, n_et * hidden), BF16),
        ),
        in_specs=[pl.BlockSpec(memory_space=pltpu.HBM)] * 6,
        out_specs=(vmem, vmem, vmem),
        scratch_shapes=[
            pltpu.VMEM((n_ep, 2, tokens, half), BF16),
            pltpu.VMEM((n_ep, 2, 8, tokens), F32),
            pltpu.VMEM((2, n_ep, cap, half), BF16),
            pltpu.VMEM((2, n_ep, cap, half), BF16),
            pltpu.VMEM((n_ep, cap, half), BF16),
            pltpu.VMEM((n_et, feats, hidden), BF16),
            pltpu.VMEM((2, n_et, slots, hidden), BF16),
            pltpu.VMEM((n_ep, n_et, cap, hidden), BF16),
            pltpu.VMEM((n_ep, n_et, cap, hidden), BF16),
            pltpu.VMEM((n_et, half, hidden), F32),
            pltpu.VMEM((hidden, slots), F32),
            pltpu.VMEM((hidden, slots), F32),
            pltpu.VMEM((slots, hidden), F32),
            pltpu.VMEM((width, tokens), F32),
            pltpu.VMEM((width, tokens), jnp.int32),
            pltpu.VMEM((hidden, slots), BF16),
            pltpu.VMEM((hidden, slots), BF16),
            dma((n_et,)),
            dma((6,)),
            dma((n_ep, 2)),
            dma((n_ep, 2)),
            dma((n_ep,)),
            dma((n_ep,)),
            dma((2, n_ep)),
            dma((2, n_ep)),
            dma((n_ep,)),
            dma((n_ep,)),
            dma((7,)),
            dma((7,)),
            dma((n_ep, n_et)),
            dma((n_ep, n_et)),
        ],
        compiler_params=pltpu.CompilerParams(
            collective_id=0, has_side_effects=True, vmem_limit_bytes=60 * 2**20
        ),
    )(grad_out, combine.T, routing.T, expert_down_matrix[0], gate_pre[0, 0], up_pre[0, 0])
    return gg[None, None], ug[None, None], gd[None]


def plain(n_ep, grad_out, combine, routing, expert_down_matrix, gate_pre, up_pre):
    slot_count = gate_pre.shape[-1]
    cap = slot_count // n_ep
    tokens, feats = grad_out.shape
    width = routing.shape[1]
    pairs = tokens * width
    targets = routing.reshape(pairs)
    onehot = targets[:, None] == jnp.arange(n_ep, dtype=jnp.int32)[None, :]
    place = jnp.arange(pairs, dtype=jnp.int32)
    before = (place[None, :] < place[:, None]).astype(BF16)
    counts = jnp.dot(before, onehot.astype(BF16), preferred_element_type=F32)
    ranking = jnp.sum(jnp.where(onehot, counts, 0.0), axis=1).astype(jnp.int32)
    destination = targets * cap + ranking
    matches = destination[None, :] == jnp.arange(slot_count, dtype=jnp.int32)[:, None]
    filled = jnp.any(matches, axis=1)
    source = jnp.sum(jnp.where(matches, place[None, :], 0), axis=1, dtype=jnp.int32)
    scale = jnp.take(combine.reshape(pairs), source)
    rows = jnp.take(grad_out, source // width, axis=0).astype(F32)
    outgoing = jnp.where(filled[:, None], (rows * scale[:, None]).astype(BF16), jnp.zeros((), BF16))
    incoming = lax.all_to_all(
        outgoing.reshape(n_ep, cap, feats), "ep", split_axis=0, concat_axis=0, tiled=True
    ).reshape(slot_count, feats)
    act_grad = lax.psum_scatter(
        lax.dot_general(
            expert_down_matrix[0], incoming, (((0,), (1,)), ((), ())), preferred_element_type=F32
        ).astype(BF16),
        "et",
        scatter_dimension=0,
        tiled=True,
    ).astype(F32)
    h, u = gate_pre[0, 0].astype(F32), up_pre[0, 0].astype(F32)
    sig = jax.nn.sigmoid(h)
    grad_gate = (act_grad * u * sig * (1.0 + h * (1.0 - sig))).astype(BF16)
    up_grad = (act_grad * h * sig).astype(BF16)
    activation = (h * sig * u).astype(BF16)
    part = lax.dot_general(
        incoming,
        lax.all_gather(activation, "et", axis=0, tiled=True),
        (((0,), (1,)), ((), ())),
        preferred_element_type=F32,
    ).astype(BF16)
    grad_down = lax.psum_scatter(part, "rep", scatter_dimension=0, tiled=True)
    return grad_gate[None, None], up_grad[None, None], grad_down[None]


def solution(mesh):
    n_ep, n_et, n_rep = mesh.shape["ep"], mesh.shape["et"], mesh.shape["rep"]

    def local(grad_out, combine, routing, expert_down_matrix, gate_pre, up_pre):
        args = (grad_out, combine, routing, expert_down_matrix, gate_pre, up_pre)
        whole_tiles = gate_pre.shape[-1] // n_ep % 16 == 0
        if n_ep == 4 and n_et == 4 and n_rep == 2 and whole_tiles:
            return fused(n_ep, n_et, *args)
        return plain(n_ep, *args)

    return jax.shard_map(
        local,
        mesh=mesh,
        in_specs=(
            P(("ep", "rep"), "et"),
            P(("ep", "rep"), None),
            P(("ep", "rep"), None),
            P("ep", "et", None),
            P("ep", "rep", "et", None),
            P("ep", "rep", "et", None),
        ),
        out_specs=(
            P("ep", "rep", "et", None),
            P("ep", "rep", "et", None),
            P("ep", ("et", "rep"), None),
        ),
        check_vma=False,
    )
```

time: 86.5 us -> 71.4 us (0.83)
  the two profiles are of different devices: /device:TPU:16 before, /device:TPU:0 now
where the time goes in v2:
time: 71.4 us; the launch traced here: 70.9 us
  Pallas kernels  63.9 us (89%)
  local copies, waits for them, and re-layouts  6.4 us (9%)
    pallas_call x1, Pallas kernels, fused(): pl.pallas_call(functools.partial(kernel, n_ep, n_et), out_shape=(jax.Shap...  63.9 us
    unnamed x3, local copies, waits for them, and re-layouts  6.4 us

profile of v2, /device:TPU:0, one launch (start us, length us, event | category | flops | bytes accessed | tf_op | source)
XLA Modules:
  0.0 70.9 jit_solution(14473471735655655232)
XLA Ops:
  0.6 63.9 %shard_map.85 = (bf16[256,768]{1,0:T(8,128)(2,1)}, bf16[256,768]{1,0:T(8,128)(2,1)}, bf16[896,1024]{1,0:T(8,128)(2,1)}) custom-call(bf16[256,1792]{1,0:T(8,128)(2,1)} %grad_hbm.1, f32[2,256]{1,0:T(2,128)} %bitcast.14, s32[2,256]{1,0:T(2,128)} %bitcast.15, bf16[1792,1024]{1,0:T(8,128)(2,1)} %bitcast.8, bf16[256,768]{1,0:T(8,128)(2,1)} %bitcast.10, ...), custom_call_target="tpu_custom_call" | custom-call | tf_op jit(solution)/shard_map/pallas_call | solution.py:330
  64.5 1.8 %copy.12 = bf16[1,1,256,768]{3,2,1,0:T(8,128)(2,1)} copy(bf16[1,1,256,768]{3,2,1,0:T(8,128)(2,1)} %bitcast.13) | data formatting | bytes 786432
  66.3 1.8 %copy.13 = bf16[1,1,256,768]{3,2,1,0:T(8,128)(2,1)} copy(bf16[1,1,256,768]{3,2,1,0:T(8,128)(2,1)} %bitcast.12) | data formatting | bytes 786432
  68.1 2.9 %copy.14 = bf16[1,896,1024]{2,1,0:T(8,128)(2,1)} copy(bf16[1,896,1024]{2,1,0:T(8,128)(2,1)} %bitcast.9) | data formatting | bytes 3670016

commit v3 on v2

--- a/solution.py
+++ b/solution.py
@@ -16,8 +16,8 @@
     n_ep, n_et, grad_hbm, comb_hbm, route_hbm, down_ref, gate_hbm, up_hbm,
     gg_ref, ug_ref, gd_ref,
     tok_buf, meta_buf, out_buf, in_buf, y_buf, weight, act_buf, part_buf, sum_buf, total,
-    coef_g, coef_u, act_grad, comb_ref, route_ref, gate_ref, up_ref,
-    w_sem, l_sem, t_send, t_recv, m_send, m_recv,
+    coef_g, coef_u, act_grad, begun, comb_ref, route_ref, gate_ref, up_ref,
+    w_sem, l_sem, t_send, t_recv, c_send, c_recv, m_send, m_recv,
     z_send, z_recv, y_send, y_recv, a_send, a_recv, p_send, p_recv,
 ):
     ep, et, rep = lax.axis_index("ep"), lax.axis_index("et"), lax.axis_index("rep")
@@ -60,7 +60,7 @@
             barrier, inc=1, device_id={"et": lax.rem(et + k, n_et)}, device_id_type=MESH
         )
     pl.semaphore_signal(barrier, inc=1, device_id={"rep": other}, device_id_type=MESH)
-    for i in (2, 3, 0, 1, 4, 5):
+    for i in (0, 1, 2, 3, 4, 5):
         load(i).start()
     for t in range(n_et):
         load_w(t).start()
@@ -75,6 +75,29 @@
             device_id_type=MESH,
         )
 
+    cuts = (pl.ds(0, half // 256 * 128 + 128), pl.ds(half // 256 * 128 + 128, half - half // 256 * 128 - 128))
+
+    def t_piece(source, j):
+        piece = tok_buf.at[source, rep, :, cuts[j]]
+        return pltpu.make_async_remote_copy(
+            src_ref=piece,
+            dst_ref=piece,
+            send_sem=c_send.at[j],
+            recv_sem=c_recv.at[j],
+            device_id={"ep": onward},
+            device_id_type=MESH,
+        )
+
+    def z_piece(source, j):
+        return pltpu.make_async_remote_copy(
+            src_ref=out_buf.at[rep, source, :, cuts[j]],
+            dst_ref=in_buf.at[rep, source, :, cuts[j]],
+            send_sem=c_send.at[2 + j],
+            recv_sem=c_recv.at[2 + j],
+            device_id={"ep": near},
+            device_id_type=MESH,
+        )
+
     def m_copy(source):
         return pltpu.make_async_remote_copy(
             src_ref=meta_buf.at[source],
@@ -124,6 +147,11 @@
             device_id={"et": t},
             device_id_type=MESH,
         )
+
+    pl.semaphore_wait(barrier, n_ep - 1 + n_et - 1 + 1)
+    for i, h in enumerate((other, rep)):
+        load(i).wait()
+        t_copy(ep, h).start()
 
     load(2).wait()
     load(3).wait()
@@ -144,7 +172,7 @@
     meta_buf[ep, 1] = jnp.where(first, comb_ref[0:1, :], comb_ref[1:2, :])
     places = lax.broadcasted_iota(jnp.int32, (cap, tokens), 0).astype(F32)
 
-    def routed(source, h, expert):
+    def routed(source, h, expert, columns=slice(None)):
         chosen = meta_buf[source, 0, pl.ds(expert, 1), :] == places
         scale = jnp.sum(
             jnp.where(chosen, meta_buf[source, 1, pl.ds(expert, 1), :], 0.0),
@@ -153,16 +181,12 @@
         )
         picked = jnp.dot(
             jnp.where(chosen, 1.0, 0.0).astype(BF16),
-            tok_buf[source, h],
+            tok_buf[source, h, :, columns],
             preferred_element_type=F32,
         )
         return (picked * scale).astype(BF16)
 
-    pl.semaphore_wait(barrier, n_ep - 1 + n_et - 1 + 1)
     m_copy(ep).start()
-    for i, h in enumerate((other, rep)):
-        load(i).wait()
-        t_copy(ep, h).start()
 
     def pass_slots(source, h):
         out_buf[h, source] = routed(source, h, near)
@@ -190,23 +214,35 @@
     coef_g[...] = u_value * sig * (1.0 + h_value * (1.0 - sig))
     coef_u[...] = silu
 
-    def partial(source):
+    def product(h, source, t):
+        return jnp.dot(
+            in_buf[h, source],
+            weight[t, pl.ds(pl.multiple_of(h * half, 128), half)],
+            preferred_element_type=F32,
+        )
+
+    def begin(source):
+        def one(t, carry):
+            begun[t] = product(other, source, t)
+            return carry
+
+        lax.fori_loop(0, n_et, one, 0)
+
+    def partial(source, is_begun=False):
         def one(k, carry):
-            t = lax.rem(et + k, n_et)
-            value = jnp.dot(
-                in_buf[0, source], weight[t, pl.ds(0, half)], preferred_element_type=F32
-            ) + jnp.dot(
-                in_buf[1, source], weight[t, pl.ds(half, half)], preferred_element_type=F32
-            )
+            base = et + lax.rem((k + 1) // 2, 2) * (beside - et)
+            t = lax.rem(base + 2 * (1 - k // 2), n_et)
+            value = product(rep, source, t)
+            value = value + (begun[t] if is_begun else product(other, source, t))
             part_buf[source, t] = value.astype(BF16)
 
-            @pl.when(k < n_et)
+            @pl.when(k < n_et - 1)
             def _():
                 p_copy(source, t, et).start()
 
             return carry
 
-        lax.fori_loop(1, n_et + 1, one, 0)
+        lax.fori_loop(0, n_et, one, 0)
 
     def weigh(slots_ref, r, source, start=False):
         turned = slots_ref[...].T
@@ -243,7 +279,10 @@
             if which == 0:
                 if h is other:
                     m_copy(source).start()
-                t_copy(source, h).start()
+                    t_copy(source, h).start()
+                else:
+                    for j in range(2):
+                        t_piece(source, j).start()
             else:
                 pass_slots(source, h)
             in_buf[h, source] = routed(source, h, ep)
@@ -254,6 +293,20 @@
 
         if h is other:
             y_copy(source).start()
+
+    def arrive_last():
+        @pl.when(is_inner)
+        def _():
+            for j in range(2):
+                t_piece(third, j).wait_recv()
+                out_buf[rep, third, :, cuts[j]] = routed(third, rep, near, cuts[j])
+                z_piece(third, j).start()
+            in_buf[rep, third] = routed(third, rep, ep)
+
+        @pl.when(inner == 0)
+        def _():
+            for j in range(2):
+                z_piece(third, j).wait_recv()
 
     for t in range(n_et):
         load_w(t).wait()
@@ -285,8 +338,9 @@
     weigh_y(near)
     weigh_own(second)
     gather(second)
-    arrive(2, rep)
-    partial(third)
+    begin(third)
+    arrive_last()
+    partial(third, True)
     weigh_y(second)
     weigh_own(third)
     weigh_y(third)
@@ -310,9 +364,13 @@
     def _():
         m_copy(near).wait_send()
         for h in (other, rep):
-            t_copy(near, h).wait_send()
-            for source in (ep, second, third):
+            for source in (ep, second):
                 z_copy(source, h).wait_send()
+        t_copy(near, other).wait_send()
+        z_copy(third, other).wait_send()
+        for j in range(2):
+            t_piece(near, j).wait_send()
+            z_piece(third, j).wait_send()
 
     for source in (ep, near, second, third):
         y_copy(source).wait_send()
@@ -350,6 +408,7 @@
             pltpu.VMEM((hidden, slots), F32),
             pltpu.VMEM((hidden, slots), F32),
             pltpu.VMEM((slots, hidden), F32),
+            pltpu.VMEM((n_et, cap, hidden), F32),
             pltpu.VMEM((width, tokens), F32),
             pltpu.VMEM((width, tokens), jnp.int32),
             pltpu.VMEM((hidden, slots), BF16),
@@ -358,6 +417,8 @@
             dma((6,)),
             dma((n_ep, 2)),
             dma((n_ep, 2)),
+            dma((4,)),
+            dma((4,)),
             dma((n_ep,)),
             dma((n_ep,)),
             dma((2, n_ep)),
@@ -373,7 +434,39 @@
             collective_id=0, has_side_effects=True, vmem_limit_bytes=60 * 2**20
         ),
     )(grad_out, combine.T, routing.T, expert_down_matrix[0], gate_pre[0, 0], up_pre[0, 0])
+    gg, ug, gd = hand_over(gg, ug, gd)
     return gg[None, None], ug[None, None], gd[None]
+
+
+def hand_over(*arrays):
+    pieces = 4
+
+    def copy_kernel(*refs):
+        count = len(arrays)
+        sems = refs[-1]
+        copies = []
+        for i in range(count):
+            step = arrays[i].shape[0] // pieces
+            for j in range(pieces):
+                rows = pl.ds(j * step, step)
+                copies.append(
+                    pltpu.make_async_copy(
+                        refs[i].at[rows], refs[count + i].at[rows], sems.at[i, j]
+                    )
+                )
+        for copy in copies:
+            copy.start()
+        for copy in copies:
+            copy.wait()
+
+    anywhere = pl.BlockSpec(memory_space=pl.ANY)
+    return pl.pallas_call(
+        copy_kernel,
+        out_shape=tuple(jax.ShapeDtypeStruct(a.shape, a.dtype) for a in arrays),
+        in_specs=[anywhere] * len(arrays),
+        out_specs=(anywhere,) * len(arrays),
+        scratch_shapes=[pltpu.SemaphoreType.DMA((len(arrays), pieces))],
+    )(*arrays)
 
 
 def plain(n_ep, grad_out, combine, routing, expert_down_matrix, gate_pre, up_pre):

time: 71.4 us -> 151 us (2.11)
  Pallas kernels: 63.9 us -> 150 us
  local copies, waits for them, and re-layouts: 6.4 us -> 0 us
    pallas_call x0 -> x1, Pallas kernels: none -> 80.6 us  [hand_over(): pl.pallas_call(copy_kernel, out_shape=tuple((jax.ShapeDtypeStruct(a.shape...]
    unnamed x3 -> x0, local copies, waits for them, and re-layouts: 6.4 us -> none
    pallas_call x1, Pallas kernels: 63.9 us -> 69.3 us  [fused(): pl.pallas_call(functools.partial(kernel, n_ep, n_et), out_shape=(jax.Shap...]
where the time goes in v3:
time: 151 us
  Pallas kernels  150 us (99%)
    pallas_call x1, Pallas kernels, hand_over(): pl.pallas_call(copy_kernel, out_shape=tuple((jax.ShapeDtypeStruct(a.shape...  80.6 us
    pallas_call x1, Pallas kernels, fused(): pl.pallas_call(functools.partial(kernel, n_ep, n_et), out_shape=(jax.Shap...  69.3 us

profile of v3, /device:TPU:0, one launch (start us, length us, event | category | flops | bytes accessed | tf_op | source)
XLA Modules:
  0.0 150.6 jit_solution(13263213559576088115)
XLA Ops:
  0.6 69.3 %shard_map.85 = (bf16[256,768]{1,0:T(8,128)(2,1)}, bf16[256,768]{1,0:T(8,128)(2,1)}, bf16[896,1024]{1,0:T(8,128)(2,1)}) custom-call(bf16[256,1792]{1,0:T(8,128)(2,1)} %grad_hbm.1, f32[2,256]{1,0:T(2,128)} %bitcast.11, s32[2,256]{1,0:T(2,128)} %bitcast.12, bf16[1792,1024]{1,0:T(8,128)(2,1)} %bitcast.8, bf16[256,768]{1,0:T(8,128)(2,1)} %bitcast.9, ...), custom_call_target="tpu_custom_call" | custom-call | tf_op jit(solution)/shard_map/pallas_call | solution.py:388
  69.9 80.6 %shard_map.86 = (bf16[256,768]{1,0:T(8,128)(2,1)}, bf16[256,768]{1,0:T(8,128)(2,1)}, bf16[896,1024]{1,0:T(8,128)(2,1)}) custom-call(bf16[256,768]{1,0:T(8,128)(2,1)} %get-tuple-element.9.refs_0_, bf16[256,768]{1,0:T(8,128)(2,1)} %get-tuple-element.10.refs_1_, bf16[896,1024]{1,0:T(8,128)(2,1)} %get-tuple-element.11.refs_2_), custom_call_target="tpu_custom_call" | custom-call | tf_op jit(solution)/shard_map/pallas_call | solution.py:463

commit v4 on v3

--- a/solution.py
+++ b/solution.py
@@ -149,9 +149,8 @@
         )
 
     pl.semaphore_wait(barrier, n_ep - 1 + n_et - 1 + 1)
-    for i, h in enumerate((other, rep)):
-        load(i).wait()
-        t_copy(ep, h).start()
+    load(0).wait()
+    t_copy(ep, other).start()
 
     load(2).wait()
     load(3).wait()
@@ -187,6 +186,8 @@
         return (picked * scale).astype(BF16)
 
     m_copy(ep).start()
+    load(1).wait()
+    t_copy(ep, rep).start()
 
     def pass_slots(source, h):
         out_buf[h, source] = routed(source, h, near)
@@ -443,29 +444,36 @@
 
     def copy_kernel(*refs):
         count = len(arrays)
-        sems = refs[-1]
-        copies = []
+        taken, given, held = refs[:count], refs[count:2 * count], refs[2 * count:3 * count]
+        in_sems, out_sems = refs[3 * count:]
+        loads, stores = [], []
         for i in range(count):
             step = arrays[i].shape[0] // pieces
             for j in range(pieces):
                 rows = pl.ds(j * step, step)
-                copies.append(
-                    pltpu.make_async_copy(
-                        refs[i].at[rows], refs[count + i].at[rows], sems.at[i, j]
-                    )
+                loads.append(
+                    pltpu.make_async_copy(taken[i].at[rows], held[i].at[rows], in_sems.at[i, j])
                 )
-        for copy in copies:
-            copy.start()
-        for copy in copies:
-            copy.wait()
-
-    anywhere = pl.BlockSpec(memory_space=pl.ANY)
+                stores.append(
+                    pltpu.make_async_copy(held[i].at[rows], given[i].at[rows], out_sems.at[i, j])
+                )
+        for load in loads:
+            load.start()
+        for load, store in zip(loads, stores):
+            load.wait()
+            store.start()
+        for store in stores:
+            store.wait()
+
+    far = pl.BlockSpec(memory_space=pltpu.HBM)
+    sems = pltpu.SemaphoreType.DMA((len(arrays), pieces))
     return pl.pallas_call(
         copy_kernel,
         out_shape=tuple(jax.ShapeDtypeStruct(a.shape, a.dtype) for a in arrays),
-        in_specs=[anywhere] * len(arrays),
-        out_specs=(anywhere,) * len(arrays),
-        scratch_shapes=[pltpu.SemaphoreType.DMA((len(arrays), pieces))],
+        in_specs=[far] * len(arrays),
+        out_specs=(far,) * len(arrays),
+        scratch_shapes=[pltpu.VMEM(a.shape, a.dtype) for a in arrays] + [sems, sems],
+        compiler_params=pltpu.CompilerParams(vmem_limit_bytes=60 * 2**20),
     )(*arrays)
 
 

time: 151 us -> 68.5 us (0.45)
  Pallas kernels: 150 us -> 67.7 us
    pallas_call x1, Pallas kernels: 80.6 us -> 2.8 us  [hand_over(): pl.pallas_call(copy_kernel, out_shape=tuple((jax.ShapeDtypeStruct(a.shape...]
    pallas_call x1, Pallas kernels: 69.3 us -> 64.9 us  [fused(): pl.pallas_call(functools.partial(kernel, n_ep, n_et), out_shape=(jax.Shap...]
where the time goes in v4:
time: 68.5 us; the launch traced here: 68.4 us
  Pallas kernels  67.7 us (99%)
    pallas_call x1, Pallas kernels, fused(): pl.pallas_call(functools.partial(kernel, n_ep, n_et), out_shape=(jax.Shap...  64.9 us
    pallas_call x1, Pallas kernels, hand_over(): pl.pallas_call(copy_kernel, out_shape=tuple((jax.ShapeDtypeStruct(a.shape...  2.8 us

profile of v4, /device:TPU:0, one launch (start us, length us, event | category | flops | bytes accessed | tf_op | source)
XLA Modules:
  0.0 68.4 jit_solution(541294182050417646)
XLA Ops:
  0.6 64.9 %shard_map.85 = (bf16[256,768]{1,0:T(8,128)(2,1)}, bf16[256,768]{1,0:T(8,128)(2,1)}, bf16[896,1024]{1,0:T(8,128)(2,1)}) custom-call(bf16[256,1792]{1,0:T(8,128)(2,1)} %grad_hbm.1, f32[2,256]{1,0:T(2,128)} %bitcast.11, s32[2,256]{1,0:T(2,128)} %bitcast.12, bf16[1792,1024]{1,0:T(8,128)(2,1)} %bitcast.8, bf16[256,768]{1,0:T(8,128)(2,1)} %bitcast.9, ...), custom_call_target="tpu_custom_call" | custom-call | tf_op jit(solution)/shard_map/pallas_call | solution.py:389
  65.6 2.8 %shard_map.86 = (bf16[256,768]{1,0:T(8,128)(2,1)}, bf16[256,768]{1,0:T(8,128)(2,1)}, bf16[896,1024]{1,0:T(8,128)(2,1)}) custom-call(bf16[256,768]{1,0:T(8,128)(2,1)} %get-tuple-element.9.refs_0_, bf16[256,768]{1,0:T(8,128)(2,1)} %get-tuple-element.10.refs_1_, bf16[896,1024]{1,0:T(8,128)(2,1)} %get-tuple-element.11.refs_2_), custom_call_target="tpu_custom_call" | custom-call | tf_op jit(solution)/shard_map/pallas_call | solution.py:470

commit v5 on v4

--- a/solution.py
+++ b/solution.py
@@ -17,7 +17,7 @@
     gg_ref, ug_ref, gd_ref,
     tok_buf, meta_buf, out_buf, in_buf, y_buf, weight, act_buf, part_buf, sum_buf, total,
     coef_g, coef_u, act_grad, begun, comb_ref, route_ref, gate_ref, up_ref,
-    w_sem, l_sem, t_send, t_recv, c_send, c_recv, m_send, m_recv,
+    w_sem, l_sem, t_send, t_recv, m_send, m_recv,
     z_send, z_recv, y_send, y_recv, a_send, a_recv, p_send, p_recv,
 ):
     ep, et, rep = lax.axis_index("ep"), lax.axis_index("et"), lax.axis_index("rep")
@@ -72,29 +72,6 @@
             send_sem=t_send.at[source, h],
             recv_sem=t_recv.at[source, h],
             device_id={"ep": onward},
-            device_id_type=MESH,
-        )
-
-    cuts = (pl.ds(0, half // 256 * 128 + 128), pl.ds(half // 256 * 128 + 128, half - half // 256 * 128 - 128))
-
-    def t_piece(source, j):
-        piece = tok_buf.at[source, rep, :, cuts[j]]
-        return pltpu.make_async_remote_copy(
-            src_ref=piece,
-            dst_ref=piece,
-            send_sem=c_send.at[j],
-            recv_sem=c_recv.at[j],
-            device_id={"ep": onward},
-            device_id_type=MESH,
-        )
-
-    def z_piece(source, j):
-        return pltpu.make_async_remote_copy(
-            src_ref=out_buf.at[rep, source, :, cuts[j]],
-            dst_ref=in_buf.at[rep, source, :, cuts[j]],
-            send_sem=c_send.at[2 + j],
-            recv_sem=c_recv.at[2 + j],
-            device_id={"ep": near},
             device_id_type=MESH,
         )
 
@@ -280,10 +257,7 @@
             if which == 0:
                 if h is other:
                     m_copy(source).start()
-                    t_copy(source, h).start()
-                else:
-                    for j in range(2):
-                        t_piece(source, j).start()
+                t_copy(source, h).start()
             else:
                 pass_slots(source, h)
             in_buf[h, source] = routed(source, h, ep)
@@ -294,20 +268,6 @@
 
         if h is other:
             y_copy(source).start()
-
-    def arrive_last():
-        @pl.when(is_inner)
-        def _():
-            for j in range(2):
-                t_piece(third, j).wait_recv()
-                out_buf[rep, third, :, cuts[j]] = routed(third, rep, near, cuts[j])
-                z_piece(third, j).start()
-            in_buf[rep, third] = routed(third, rep, ep)
-
-        @pl.when(inner == 0)
-        def _():
-            for j in range(2):
-                z_piece(third, j).wait_recv()
 
     for t in range(n_et):
         load_w(t).wait()
@@ -340,7 +300,7 @@
     weigh_own(second)
     gather(second)
     begin(third)
-    arrive_last()
+    arrive(2, rep)
     partial(third, True)
     weigh_y(second)
     weigh_own(third)
@@ -365,13 +325,9 @@
     def _():
         m_copy(near).wait_send()
         for h in (other, rep):
-            for source in (ep, second):
+            t_copy(near, h).wait_send()
+            for source in (ep, second, third):
                 z_copy(source, h).wait_send()
-        t_copy(near, other).wait_send()
-        z_copy(third, other).wait_send()
-        for j in range(2):
-            t_piece(near, j).wait_send()
-            z_piece(third, j).wait_send()
 
     for source in (ep, near, second, third):
         y_copy(source).wait_send()
@@ -418,8 +374,6 @@
             dma((6,)),
             dma((n_ep, 2)),
             dma((n_ep, 2)),
-            dma((4,)),
-            dma((4,)),
             dma((n_ep,)),
             dma((n_ep,)),
             dma((2, n_ep)),

time: 68.5 us -> 67.6 us (0.987)
  Pallas kernels: 67.7 us -> 66.8 us
    pallas_call x1, Pallas kernels: 64.9 us -> 64 us  [fused(): pl.pallas_call(functools.partial(kernel, n_ep, n_et), out_shape=(jax.Shap...]
where the time goes in v5:
time: 67.6 us; the launch traced here: 67.4 us
  Pallas kernels  66.8 us (99%)
    pallas_call x1, Pallas kernels, fused(): pl.pallas_call(functools.partial(kernel, n_ep, n_et), out_shape=(jax.Shap...  64 us
    pallas_call x1, Pallas kernels, hand_over(): pl.pallas_call(copy_kernel, out_shape=tuple((jax.ShapeDtypeStruct(a.shape...  2.8 us

profile of v5, /device:TPU:0, one launch (start us, length us, event | category | flops | bytes accessed | tf_op | source)
XLA Modules:
  0.0 67.4 jit_solution(17822971878301026571)
XLA Ops:
  0.6 64.0 %shard_map.85 = (bf16[256,768]{1,0:T(8,128)(2,1)}, bf16[256,768]{1,0:T(8,128)(2,1)}, bf16[896,1024]{1,0:T(8,128)(2,1)}) custom-call(bf16[256,1792]{1,0:T(8,128)(2,1)} %grad_hbm.1, f32[2,256]{1,0:T(2,128)} %bitcast.11, s32[2,256]{1,0:T(2,128)} %bitcast.12, bf16[1792,1024]{1,0:T(8,128)(2,1)} %bitcast.8, bf16[256,768]{1,0:T(8,128)(2,1)} %bitcast.9, ...), custom_call_target="tpu_custom_call" | custom-call | tf_op jit(solution)/shard_map/pallas_call | solution.py:345
  64.6 2.8 %shard_map.86 = (bf16[256,768]{1,0:T(8,128)(2,1)}, bf16[256,768]{1,0:T(8,128)(2,1)}, bf16[896,1024]{1,0:T(8,128)(2,1)}) custom-call(bf16[256,768]{1,0:T(8,128)(2,1)} %get-tuple-element.9.refs_0_, bf16[256,768]{1,0:T(8,128)(2,1)} %get-tuple-element.10.refs_1_, bf16[896,1024]{1,0:T(8,128)(2,1)} %get-tuple-element.11.refs_2_), custom_call_target="tpu_custom_call" | custom-call | tf_op jit(solution)/shard_map/pallas_call | solution.py:424
